TPU v7x, 32 devices: a whole 2x2x4 slice. The times are simulated.
32 devices in a mesh: samp: 8 (over z, y), feat: 4 (over x, core).
Axes of the slice: x: 2, y: 2, z: 4, core: 2. Of those that a mesh axis runs over, the one named last changes fastest.
Arguments:
- states: bfloat16 [8192, 16384], P('samp', 'feat'), may hold values from -0.176776695 to 0.176776695
- targets: float32 [8192, 128], P('samp'), may hold values from -40 to 40
- penalty: float32 [128], replicated, may hold values from 0.1 to 1
Outputs:
- readout: float32 [16384, 128], P('feat')
- residual: float32 [8192, 128], P('samp')
All inputs are finite; a program needn't handle non-finite values.
Results may differ from a plain program's by a relative error of at most 0.0058.
Values may be sent and summed in bfloat16 or wider, within the bound.
A program may use at most 64 MiB of HBM per device.

v0:
```python
import jax
import jax.numpy as jnp
from jax import lax
from jax.sharding import PartitionSpec as P

ITERS = 3


def shards(states, targets, penalty):
    feat_rows = states.shape[1]

    def weight_sum(value):
        return lax.psum(value, "feat")

    def gradient_of(residual, readout):
        residual_b = residual.astype(jnp.bfloat16)
        partial_value = lax.dot_general(
            states, residual_b, (((0,), (0,)), ((), ())), preferred_element_type=jnp.float32
        )
        summed = lax.psum(partial_value, "samp")
        return summed - penalty * readout

    readout = jnp.zeros((feat_rows, targets.shape[1]), jnp.float32)
    residual = targets
    gradient = gradient_of(residual, readout)
    direction = gradient
    norm_now = weight_sum(jnp.sum(gradient * gradient, axis=0))
    for step in range(ITERS):
        direction_b = direction.astype(jnp.bfloat16)
        image_partial_value = jnp.dot(states, direction_b, preferred_element_type=jnp.float32)
        image = lax.psum(image_partial_value, "feat")
        image_sq = jnp.sum(image * image, axis=0)
        direction_sq = jnp.sum(direction * direction, axis=0)
        curvature = lax.psum(image_sq, "samp") + penalty * weight_sum(direction_sq)
        step_size = norm_now / curvature
        readout = readout + step_size * direction
        residual = residual - step_size * image
        if step + 1 < ITERS:
            gradient = gradient_of(residual, readout)
            norm_next = weight_sum(jnp.sum(gradient * gradient, axis=0))
            direction = gradient + norm_next / norm_now * direction
            norm_now = norm_next
    return (readout, residual)


def solution(mesh):
    in_specs = (P("samp", "feat"), P("samp", None), P())
    out_specs = (P("feat", None), P("samp", None))
    return jax.shard_map(shards, mesh=mesh, in_specs=in_specs, out_specs=out_specs, check_vma=False)
```

profile of v0, /device:TPU:0, one launch (start us, length us, event | category | flops | bytes accessed | tf_op | source)
XLA Modules:
  0.0 558.5 jit_solution(16675980969986547672)
XLA Ops:
  7.2 0.0 all-reduce.7.cloned.1.call-start
  7.2 7.1 %fusion.5 = f32[4096,128]{1,0:T(8,128)} fusion(bf16[1024,4096]{1,0:T(8,128)(2,1)} %param.3, f32[1024,128]{1,0:T(8,128)} %param.4), kind=kOutput, calls=%fused_computation.28 | convolution fusion | flops 1073872896 | bytes 11010048 | tf_op jit(solution)/shard_map/dot_general | solution.py:17
  14.3 0.0 copy-start.6
  14.3 0.0 all-reduce.7.cloned.1.call-update
  14.4 0.0 all-reduce.9.cloned.1.call-start
  14.4 0.6 copy-done.6
  15.0 0.0 copy-start.5
  15.0 104.0 %all-reduce.7.cloned.1.call-done = f32[4096,128]{1,0:T(8,128)} async-done(((f32[4096,128]{1,0:T(8,128)}), f32[4096,128]{1,0:T(8,128)}) %all-reduce.7.cloned.1.call-update) | async-done | bytes 2097168 | tf_op jit(solution)/shard_map/psum | solution.py:20
  119.0 0.0 copy-start
  119.0 7.8 %convolution_bitcast_fusion.4 = f32[1024,128]{0,1:T(8,128)} fusion(bf16[1024,4096]{1,0:T(8,128)(2,1)} %param.3, f32[4096,128]{1,0:T(8,128)} %all-reduce.7.cloned.1.call-done, f32[128]{0:T(128)S(1)} %broadcast_multiply_fusion), kind=kOutput, calls=%fused_computation.16 | convolution fusion | flops 1074790400 | bytes 11010560 | tf_op jit(solution)/shard_map/dot_general | solution.py:30
  126.9 0.0 all-reduce.9.cloned.1.call-update
  126.9 0.0 all-reduce.11.cloned.1.call-start
  126.9 0.0 copy-done.5
  126.9 0.2 copy.5
  127.1 0.0 copy-done
  127.2 0.6 multiply_reduce_fusion.4
  127.7 6.3 %psum.102 = f32[128]{0:T(128)S(1)} all-reduce(f32[128]{0:T(128)S(1)} %multiply_reduce_fusion.4), channel_id=1, replica_groups=mesh['samp'=8,'feat'=4] {'feat'}, use_global_device_ids=true, to_apply=%region_2.0 | all-reduce | flops 128 | bytes 1024 | tf_op jit(solution)/shard_map/psum | solution.py:13
  134.0 25.9 %all-reduce.9.cloned.1.call-done = f32[1024,128]{0,1:T(8,128)} async-done(((f32[1024,128]{0,1:T(8,128)}), f32[1024,128]{0,1:T(8,128)}) %all-reduce.9.cloned.1.call-update) | async-done | bytes 524304 | tf_op jit(solution)/shard_map/psum | solution.py:31
  159.9 1.2 multiply_reduce_fusion.7
  161.1 21.4 %psum.104 = f32[128]{0:T(128)S(1)} all-reduce(f32[128]{0:T(128)S(1)} %multiply_reduce_fusion.7), channel_id=1, replica_groups=mesh['samp'=8,'feat'=4] {'samp'}, use_global_device_ids=true, to_apply=%region_5.0 | all-reduce | flops 128 | bytes 1024 | tf_op jit(solution)/shard_map/psum | solution.py:34
  182.5 8.3 %convolution_bitcast_fusion.1 = f32[4096,128]{1,0:T(8,128)} fusion(bf16[1024,4096]{1,0:T(8,128)(2,1)} %param.3, f32[1024,128]{0,1:T(8,128)S(1)} %copy.5, f32[1024,128]{0,1:T(8,128)} %all-reduce.9.cloned.1.call-done, f32[128]{0:T(128)S(1)} %add_divide_fusion.2), kind=kOutput, calls=%fused_computation.1 | convolution fusion | flops 1074135040 | bytes 11534848 | tf_op jit(solution)/shard_map/dot_general | solution.py:17
  190.8 0.0 all-reduce.11.cloned.1.call-update
  190.8 0.0 all-reduce.13.cloned.1.call-start
  190.8 98.2 %all-reduce.11.cloned.1.call-done = f32[4096,128]{1,0:T(8,128)} async-done(((f32[4096,128]{1,0:T(8,128)}), f32[4096,128]{1,0:T(8,128)}) %all-reduce.11.cloned.1.call-update) | async-done | bytes 2097168 | tf_op jit(solution)/shard_map/psum | solution.py:20
  289.0 2.2 multiply_reduce_fusion.3
  291.1 6.5 %psum.106 = f32[128]{0:T(128)S(1)} all-reduce(f32[128]{0:T(128)S(1)} %multiply_reduce_fusion.3), channel_id=1, replica_groups=mesh['samp'=8,'feat'=4] {'feat'}, use_global_device_ids=true, to_apply=%region_8.0 | all-reduce | flops 128 | bytes 1024 | tf_op jit(solution)/shard_map/psum | solution.py:13
  297.6 7.7 %convolution_bitcast_fusion.3 = f32[1024,128]{0,1:T(8,128)} fusion(bf16[1024,4096]{1,0:T(8,128)(2,1)} %param.3, f32[4096,128]{1,0:T(8,128)} %all-reduce.11.cloned.1.call-done, f32[4096,128]{1,0:T(8,128)S(1)} %copy-done, f32[128]{0:T(128)S(1)} %div.16, f32[128]{0:T(128)S(1)} %copy-done.6, f32[128]{0:T(128)S(1)} %add_divide_fusion.2, ...), kind=kOutput, calls=%fused_computation.15 | convolution fusion | flops 1077411840 | bytes 13109248 | tf_op jit(solution)/shard_map/dot_general | solution.py:30
  305.4 0.0 all-reduce.13.cloned.1.call-update
  305.4 0.0 copy-start.2
  305.4 0.0 all-reduce.15.cloned.1.call-start
  305.4 2.2 multiply_reduce_fusion.2
  307.6 5.9 %psum.109 = f32[128]{0:T(128)S(1)} all-reduce(f32[128]{0:T(128)S(1)} %multiply_reduce_fusion.2), channel_id=1, replica_groups=mesh['samp'=8,'feat'=4] {'feat'}, use_global_device_ids=true, to_apply=%region_13.0 | all-reduce | flops 128 | bytes 1024 | tf_op jit(solution)/shard_map/psum | solution.py:13
  313.6 24.5 %all-reduce.13.cloned.1.call-done = f32[1024,128]{0,1:T(8,128)} async-done(((f32[1024,128]{0,1:T(8,128)}), f32[1024,128]{0,1:T(8,128)}) %all-reduce.13.cloned.1.call-update) | async-done | bytes 524304 | tf_op jit(solution)/shard_map/psum | solution.py:31
  338.1 1.2 multiply_reduce_fusion.6
  339.3 21.4 %psum.108 = f32[128]{0:T(128)S(1)} all-reduce(f32[128]{0:T(128)S(1)} %multiply_reduce_fusion.6), channel_id=1, replica_groups=mesh['samp'=8,'feat'=4] {'samp'}, use_global_device_ids=true, to_apply=%region_11.0 | all-reduce | flops 128 | bytes 1024 | tf_op jit(solution)/shard_map/psum | solution.py:34
  360.6 0.0 copy-done.2
  360.6 1.2 multiply_subtract_fusion.3
  361.9 0.0 copy-start.3
  361.9 0.8 copy-done.3
  362.7 8.1 %convolution_bitcast_fusion = f32[4096,128]{1,0:T(8,128)} fusion(bf16[1024,4096]{1,0:T(8,128)(2,1)} %param.3, f32[1024,128]{0,1:T(8,128)S(1)} %multiply_subtract_fusion.3), kind=kOutput, calls=%fused_computation | convolution fusion | flops 1073872896 | bytes 11010048 | tf_op jit(solution)/shard_map/dot_general | solution.py:17
  370.7 0.0 all-reduce.15.cloned.1.call-update
  370.8 0.0 all-reduce.17.cloned.1.call-start
  370.8 98.2 %all-reduce.15.cloned.1.call-done = f32[4096,128]{1,0:T(8,128)} async-done(((f32[4096,128]{1,0:T(8,128)}), f32[4096,128]{1,0:T(8,128)}) %all-reduce.15.cloned.1.call-update) | async-done | bytes 2097168 | tf_op jit(solution)/shard_map/psum | solution.py:20
  469.0 3.1 multiply_reduce_fusion.1
  472.0 6.3 %psum.111 = f32[128]{0:T(128)S(1)} all-reduce(f32[128]{0:T(128)S(1)} %multiply_reduce_fusion.1), channel_id=1, replica_groups=mesh['samp'=8,'feat'=4] {'feat'}, use_global_device_ids=true, to_apply=%region_16.0 | all-reduce | flops 128 | bytes 1024 | tf_op jit(solution)/shard_map/psum | solution.py:13
  478.4 3.2 multiply_reduce_fusion
  481.6 0.0 copy-start.1
  481.6 1.3 copy-done.1
  482.9 0.0 copy-start.4
  482.9 7.1 %convolution_bitcast_fusion.2 = f32[1024,128]{0,1:T(8,128)} fusion(bf16[1024,4096]{1,0:T(8,128)(2,1)} %param.3, f32[4096,128]{1,0:T(8,128)S(1)} %get-tuple-element.5), kind=kOutput, calls=%fused_computation.14 | convolution fusion | flops 1074266112 | bytes 11010048 | tf_op jit(solution)/shard_map/dot_general | solution.py:30
  490.0 0.0 all-reduce.17.cloned.1.call-update
  490.0 5.9 %psum.114 = f32[128]{0:T(128)S(1)} all-reduce(f32[128]{0:T(128)S(1)} %get-tuple-element.4), channel_id=1, replica_groups=mesh['samp'=8,'feat'=4] {'feat'}, use_global_device_ids=true, to_apply=%region_21.0 | all-reduce | flops 128 | bytes 1024 | tf_op jit(solution)/shard_map/psum | solution.py:13
  496.0 26.7 %all-reduce.17.cloned.1.call-done = f32[1024,128]{0,1:T(8,128)} async-done(((f32[1024,128]{0,1:T(8,128)}), f32[1024,128]{0,1:T(8,128)}) %all-reduce.17.cloned.1.call-update) | async-done | bytes 524304 | tf_op jit(solution)/shard_map/psum | solution.py:31
  522.7 1.2 multiply_reduce_fusion.5
  523.9 21.4 %psum.113 = f32[128]{0:T(128)S(1)} all-reduce(f32[128]{0:T(128)S(1)} %multiply_reduce_fusion.5), channel_id=1, replica_groups=mesh['samp'=8,'feat'=4] {'samp'}, use_global_device_ids=true, to_apply=%region_19.0 | all-reduce | flops 128 | bytes 1024 | tf_op jit(solution)/shard_map/psum | solution.py:34
  545.2 0.0 copy-done.4
  545.2 1.2 multiply_subtract_fusion.2
  546.4 1.0 copy.8
  547.4 4.2 multiply_add_fusion
  (6 shorter events, 0.0 us)
Async XLA Ops:
  7.2 111.8 %all-reduce.7.cloned.1.call-start = ((), (), s32[]{:S(2)}) async-start(), calls=%async_computation | async-start | bytes 4194304 | tf_op jit(solution)/shard_map/psum | solution.py:20
  14.3 0.7 copy-start.6
  14.4 145.6 %all-reduce.9.cloned.1.call-start = ((), (), s32[]{:S(2)}) async-start(), calls=%async_computation.1 | async-start | bytes 1048576 | tf_op jit(solution)/shard_map/psum | solution.py:31
  15.0 111.9 %copy-start.5 = (f32[1024,128]{1,0:T(8,128)S(1)}, f32[1024,128]{1,0:T(8,128)}, u32[]{:S(2)}) copy-start(f32[1024,128]{1,0:T(8,128)} %param.4) | copy-start | bytes 1572868
  119.0 8.1 %copy-start = (f32[4096,128]{1,0:T(8,128)S(1)}, f32[4096,128]{1,0:T(8,128)}, u32[]{:S(2)}) copy-start(f32[4096,128]{1,0:T(8,128)} %all-reduce.7.cloned.1.call-done) | copy-start | bytes 6291460
  126.9 162.1 %all-reduce.11.cloned.1.call-start = ((), (), s32[]{:S(2)}) async-start(), calls=%async_computation.2 | async-start | bytes 4194304 | tf_op jit(solution)/shard_map/psum | solution.py:20
  190.8 147.3 %all-reduce.13.cloned.1.call-start = ((), (), s32[]{:S(2)}) async-start(), calls=%async_computation.3 | async-start | bytes 1048576 | tf_op jit(solution)/shard_map/psum | solution.py:31
  305.4 55.3 %copy-start.2 = (f32[1024,128]{0,1:T(8,128)S(1)}, f32[1024,128]{0,1:T(8,128)}, u32[]{:S(2)}) copy-start(f32[1024,128]{0,1:T(8,128)} %all-reduce.9.cloned.1.call-done) | copy-start | bytes 1572868
  305.4 163.6 %all-reduce.15.cloned.1.call-start = ((), (), s32[]{:S(2)}) async-start(), calls=%async_computation.4 | async-start | bytes 4194304 | tf_op jit(solution)/shard_map/psum | solution.py:20
  361.9 0.8 copy-start.3
  370.8 151.9 %all-reduce.17.cloned.1.call-start = ((), (), s32[]{:S(2)}) async-start(), calls=%async_computation.5 | async-start | bytes 1048576 | tf_op jit(solution)/shard_map/psum | solution.py:31
  481.6 1.3 copy-start.1
  482.9 62.4 %copy-start.4 = (f32[1024,128]{0,1:T(8,128)S(1)}, f32[1024,128]{0,1:T(8,128)}, u32[]{:S(2)}) copy-start(f32[1024,128]{0,1:T(8,128)} %copy-done.3) | copy-start | bytes 1572868
Sparse Core Ops, SparseCore 0:
  14.5 104.4 all-reduce.6
  127.0 32.8 all-reduce.8
  190.9 98.0 all-reduce.10
  305.5 32.5 all-reduce.12
  370.9 98.0 all-reduce.14
  490.1 32.5 all-reduce.16
where the time goes:
time: 559 us; the launch traced here: 558 us
  waiting for transfers between devices  378 us (68%)
  blocking collectives  95.1 us (17%)
  matrix products  46.2 us (8%)
  other arithmetic  21.3 us (4%)
  between operations  14.2 us (3%)
    psum x3, waiting for transfers between devices, gradient_of(): summed = lax.psum(partial_value, 'samp')  300 us
    psum x3, waiting for transfers between devices, shards(): image = lax.psum(image_partial_value, 'feat')  77.2 us
    psum x3, blocking collectives, shards(): curvature = lax.psum(image_sq, 'samp') + penalty * weight_sum(direction_sq)  64.1 us
    psum x5, blocking collectives, weight_sum(): return lax.psum(value, 'feat')  31 us
    dot_general x3, matrix products, gradient_of(): lax.dot_general(states, residual_b, (((0,), (0,)), ((), ())), preferred_e...  23.5 us
    dot_general x3, matrix products, shards(): jnp.dot(states, direction_b, preferred_element_type=jnp.float32)  22.7 us
  transfers between devices with their start and end apart: 6, of which 6 were waited for; matrix products, arithmetic and copies ran while one was open for 1% of the time, Pallas kernels for 0%

commit v1 on v0

--- a/solution.py
+++ b/solution.py
@@ -28,7 +28,11 @@
     for step in range(ITERS):
         direction_b = direction.astype(jnp.bfloat16)
         image_partial_value = jnp.dot(states, direction_b, preferred_element_type=jnp.float32)
-        image = lax.psum(image_partial_value, "feat")
+        devices = lax.axis_size("feat")
+        image, far = (image_partial_value, 1)
+        while far < devices:
+            image = image + lax.ppermute(image, "feat", [(i, i ^ far) for i in range(devices)])
+            far = 2 * far
         image_sq = jnp.sum(image * image, axis=0)
         direction_sq = jnp.sum(direction * direction, axis=0)
         curvature = lax.psum(image_sq, "samp") + penalty * weight_sum(direction_sq)

time: 559 us -> 513 us (0.918)
  waiting for transfers between devices: 378 us -> 307 us
  blocking collectives: 95.1 us -> 117 us
    psum x3 -> x0, waiting for transfers between devices: 77.2 us -> none  [shards(): image = lax.psum(image_partial_value, 'feat')]
    psum x5, blocking collectives: 31 us -> 57.3 us  [weight_sum(): return lax.psum(value, 'feat')]
    ppermute x0 -> x6, waiting for transfers between devices: none -> 5.7 us  [shards(): lax.ppermute(image, 'feat', [(i, i ^ far) for i in range(devices)])]
  transfers between devices with their start and end apart: 6 -> 9, of which waited for: 6 -> 6; matrix products, arithmetic and copies ran while one was open for 1% -> 0% of each run, Pallas kernels for 0% -> 0%
where the time goes in v1:
time: 513 us
  waiting for transfers between devices  307 us (60%)
  blocking collectives  117 us (23%)
  matrix products  44.3 us (9%)
  other arithmetic  23.2 us (5%)
  between operations  13.9 us (3%)
    psum x3, waiting for transfers between devices, gradient_of(): summed = lax.psum(partial_value, 'samp')  301 us
    psum x3, blocking collectives, shards(): curvature = lax.psum(image_sq, 'samp') + penalty * weight_sum(direction_sq)  60.1 us
    psum x5, blocking collectives, weight_sum(): return lax.psum(value, 'feat')  57.3 us
    dot_general x3, matrix products, gradient_of(): lax.dot_general(states, residual_b, (((0,), (0,)), ((), ())), preferred_e...  23.3 us
    dot_general x3, matrix products, shards(): jnp.dot(states, direction_b, preferred_element_type=jnp.float32)  21 us
  transfers between devices with their start and end apart: 9, of which 6 were waited for; matrix products, arithmetic and copies ran while one was open for 0% of the time, Pallas kernels for 0%

profile of v1, /device:TPU:0, one launch (start us, length us, event | category | flops | bytes accessed | tf_op | source)
XLA Modules:
  0.0 512.6 jit_solution(5344820746191105829)
XLA Ops:
  7.2 0.0 all-reduce.4.cloned.1.call-start
  7.2 7.1 %fusion.5 = f32[4096,128]{1,0:T(8,128)} fusion(bf16[1024,4096]{1,0:T(8,128)(2,1)} %param.3, f32[1024,128]{1,0:T(8,128)} %param.4), kind=kOutput, calls=%fused_computation.28 | convolution fusion | flops 1073872896 | bytes 11010048 | tf_op jit(solution)/shard_map/dot_general | solution.py:17
  14.3 0.0 copy-start.6
  14.3 0.0 all-reduce.4.cloned.1.call-update
  14.4 0.0 all-reduce.6.cloned.1.call-start
  14.4 0.6 copy-done.6
  15.0 0.0 copy-start.5
  15.0 104.0 %all-reduce.4.cloned.1.call-done = f32[4096,128]{1,0:T(8,128)} async-done(((f32[4096,128]{1,0:T(8,128)}), f32[4096,128]{1,0:T(8,128)}) %all-reduce.4.cloned.1.call-update) | async-done | bytes 2097168 | tf_op jit(solution)/shard_map/psum | solution.py:20
  119.0 6.9 %convolution_bitcast_fusion.4 = f32[1024,128]{0,1:T(8,128)S(1)} fusion(bf16[1024,4096]{1,0:T(8,128)(2,1)} %param.3, f32[4096,128]{1,0:T(8,128)} %all-reduce.4.cloned.1.call-done, f32[128]{0:T(128)S(1)} %broadcast_multiply_fusion), kind=kOutput, calls=%fused_computation.16 | convolution fusion | flops 1074790400 | bytes 11010560 | tf_op jit(solution)/shard_map/dot_general | solution.py:30
  125.9 0.0 copy-start
  125.9 0.1 collective-permute-start
  126.0 1.9 collective-permute-done
  127.9 0.9 add.62
  128.8 1.5 collective-permute-start.1
  130.2 0.0 copy-done.5
  130.2 0.2 copy.5
  130.4 0.0 copy-done
  130.5 0.6 multiply_reduce_fusion.4
  131.0 14.6 %psum.81 = f32[128]{0:T(128)S(1)} all-reduce(f32[128]{0:T(128)S(1)} %multiply_reduce_fusion.4), channel_id=1, replica_groups=mesh['samp'=8,'feat'=4] {'feat'}, use_global_device_ids=true, to_apply=%region_2.0 | all-reduce | flops 128 | bytes 1024 | tf_op jit(solution)/shard_map/psum | solution.py:13
  145.6 0.0 collective-permute-done.1
  145.6 1.3 multiply_reduce_fusion.7
  146.9 20.0 %psum.82 = f32[128]{0:T(128)S(1)} all-reduce(f32[128]{0:T(128)S(1)} %get-tuple-element.10), channel_id=1, replica_groups=mesh['samp'=8,'feat'=4] {'samp'}, use_global_device_ids=true, to_apply=%region_4.0 | all-reduce | flops 128 | bytes 1024 | tf_op jit(solution)/shard_map/psum | solution.py:38
  167.0 8.1 %convolution_bitcast_fusion.1 = f32[4096,128]{1,0:T(8,128)} fusion(bf16[1024,4096]{1,0:T(8,128)(2,1)} %param.3, f32[1024,128]{0,1:T(8,128)S(1)} %copy.5, f32[1024,128]{0,1:T(8,128)S(1)} %get-tuple-element.11, f32[128]{0:T(128)S(1)} %add_divide_fusion.2), kind=kOutput, calls=%fused_computation.1 | convolution fusion | flops 1074135040 | bytes 11534848 | tf_op jit(solution)/shard_map/dot_general | solution.py:17
  175.1 0.0 all-reduce.6.cloned.1.call-update
  175.1 0.0 all-reduce.8.cloned.1.call-start
  175.2 98.2 %all-reduce.6.cloned.1.call-done = f32[4096,128]{1,0:T(8,128)} async-done(((f32[4096,128]{1,0:T(8,128)}), f32[4096,128]{1,0:T(8,128)}) %all-reduce.6.cloned.1.call-update) | async-done | bytes 2097168 | tf_op jit(solution)/shard_map/psum | solution.py:20
  273.4 2.2 multiply_reduce_fusion.3
  275.5 6.5 %psum.84 = f32[128]{0:T(128)S(1)} all-reduce(f32[128]{0:T(128)S(1)} %multiply_reduce_fusion.3), channel_id=1, replica_groups=mesh['samp'=8,'feat'=4] {'feat'}, use_global_device_ids=true, to_apply=%region_7.0 | all-reduce | flops 128 | bytes 1024 | tf_op jit(solution)/shard_map/psum | solution.py:13
  282.0 7.1 %convolution_bitcast_fusion.3 = f32[1024,128]{0,1:T(8,128)S(1)} fusion(bf16[1024,4096]{1,0:T(8,128)(2,1)} %param.3, f32[4096,128]{1,0:T(8,128)} %all-reduce.6.cloned.1.call-done, f32[4096,128]{1,0:T(8,128)S(1)} %copy-done, f32[128]{0:T(128)S(1)} %div.16, f32[128]{0:T(128)S(1)} %copy-done.6, f32[128]{0:T(128)S(1)} %add_divide_fusion.2, ...), kind=kOutput, calls=%fused_computation.15 | convolution fusion | flops 1077411840 | bytes 13109248 | tf_op jit(solution)/shard_map/dot_general | solution.py:30
  289.1 0.1 collective-permute-start.2
  289.2 1.9 collective-permute-done.2
  291.1 0.9 add.66
  291.9 1.1 collective-permute-start.3
  293.0 0.0 copy-done.1
  293.0 0.6 multiply_reduce_fusion.2
  293.6 14.8 %psum.86 = f32[128]{0:T(128)S(1)} all-reduce(f32[128]{0:T(128)S(1)} %multiply_reduce_fusion.2), channel_id=1, replica_groups=mesh['samp'=8,'feat'=4] {'feat'}, use_global_device_ids=true, to_apply=%region_11.0 | all-reduce | flops 128 | bytes 1024 | tf_op jit(solution)/shard_map/psum | solution.py:13
  308.3 0.0 collective-permute-done.3
  308.3 2.1 multiply_reduce_fusion.6
  310.4 20.0 %psum.85 = f32[128]{0:T(128)S(1)} all-reduce(f32[128]{0:T(128)S(1)} %get-tuple-element.8), channel_id=1, replica_groups=mesh['samp'=8,'feat'=4] {'samp'}, use_global_device_ids=true, to_apply=%region_9.0 | all-reduce | flops 128 | bytes 1024 | tf_op jit(solution)/shard_map/psum | solution.py:38
  330.4 1.2 multiply_subtract_fusion.3
  331.7 0.0 copy-start.3
  331.7 0.8 copy-done.3
  332.5 8.1 %convolution_bitcast_fusion = f32[4096,128]{1,0:T(8,128)} fusion(bf16[1024,4096]{1,0:T(8,128)(2,1)} %param.3, f32[1024,128]{0,1:T(8,128)S(1)} %multiply_subtract_fusion.3), kind=kOutput, calls=%fused_computation | convolution fusion | flops 1073872896 | bytes 11010048 | tf_op jit(solution)/shard_map/dot_general | solution.py:17
  340.5 0.0 all-reduce.8.cloned.1.call-update
  340.6 99.3 %all-reduce.8.cloned.1.call-done = f32[4096,128]{1,0:T(8,128)} async-done(((f32[4096,128]{1,0:T(8,128)}), f32[4096,128]{1,0:T(8,128)}) %all-reduce.8.cloned.1.call-update) | async-done | bytes 2097168 | tf_op jit(solution)/shard_map/psum | solution.py:20
  439.8 3.1 multiply_reduce_fusion.1
  442.9 6.3 %psum.88 = f32[128]{0:T(128)S(1)} all-reduce(f32[128]{0:T(128)S(1)} %multiply_reduce_fusion.1), channel_id=1, replica_groups=mesh['samp'=8,'feat'=4] {'feat'}, use_global_device_ids=true, to_apply=%region_14.0 | all-reduce | flops 128 | bytes 1024 | tf_op jit(solution)/shard_map/psum | solution.py:13
  449.2 3.2 multiply_reduce_fusion
  452.4 0.0 copy-start.2
  452.4 7.0 %convolution_bitcast_fusion.2 = f32[1024,128]{0,1:T(8,128)S(1)} fusion(bf16[1024,4096]{1,0:T(8,128)(2,1)} %param.3, f32[4096,128]{1,0:T(8,128)S(1)} %get-tuple-element.5), kind=kOutput, calls=%fused_computation.14 | convolution fusion | flops 1074266112 | bytes 11010048 | tf_op jit(solution)/shard_map/dot_general | solution.py:30
  459.5 0.0 copy-done.2
  459.5 0.0 copy-start.4
  459.5 0.1 collective-permute-start.4
  459.5 1.9 collective-permute-done.4
  461.4 0.1 add.71
  461.5 1.1 collective-permute-start.5
  462.6 15.1 %psum.90 = f32[128]{0:T(128)S(1)} all-reduce(f32[128]{0:T(128)S(1)} %get-tuple-element.4), channel_id=1, replica_groups=mesh['samp'=8,'feat'=4] {'feat'}, use_global_device_ids=true, to_apply=%region_18.0 | all-reduce | flops 128 | bytes 1024 | tf_op jit(solution)/shard_map/psum | solution.py:13
  477.8 0.0 collective-permute-done.5
  477.8 1.9 multiply_reduce_fusion.5
  479.7 20.0 %psum.89 = f32[128]{0:T(128)S(1)} all-reduce(f32[128]{0:T(128)S(1)} %get-tuple-element.6), channel_id=1, replica_groups=mesh['samp'=8,'feat'=4] {'samp'}, use_global_device_ids=true, to_apply=%region_16.0 | all-reduce | flops 128 | bytes 1024 | tf_op jit(solution)/shard_map/psum | solution.py:38
  499.7 0.0 copy-done.4
  499.7 1.2 multiply_subtract_fusion.2
  500.9 1.0 copy.8
  501.9 4.2 multiply_add_fusion
  (7 shorter events, 0.0 us)
Async XLA Ops:
  7.2 111.8 %all-reduce.4.cloned.1.call-start = ((), (), s32[]{:S(2)}) async-start(), calls=%async_computation | async-start | bytes 4194304 | tf_op jit(solution)/shard_map/psum | solution.py:20
  14.3 0.7 copy-start.6
  14.4 259.0 %all-reduce.6.cloned.1.call-start = ((), (), s32[]{:S(2)}) async-start(), calls=%async_computation.1 | async-start | bytes 4194304 | tf_op jit(solution)/shard_map/psum | solution.py:20
  15.0 115.2 %copy-start.5 = (f32[1024,128]{1,0:T(8,128)S(1)}, f32[1024,128]{1,0:T(8,128)}, u32[]{:S(2)}) copy-start(f32[1024,128]{1,0:T(8,128)} %param.4) | copy-start | bytes 1572868
  125.9 4.5 copy-start
  125.9 2.0 collective-permute-start
  128.8 16.8 %collective-permute-start.1 = (f32[1024,128]{0,1:T(8,128)}, f32[1024,128]{0,1:T(8,128)}, u32[]{:S(2)}, u32[]{:S(2)}) collective-permute-start(f32[1024,128]{0,1:T(8,128)} %add.62), channel_id=1, source_target_pairs={{0,2},{1,3},{2,0},{3,1},{4,6},{5,7},{6,4},{7,5},{8,10},{9,11},{10,... | collective-permute-start | bytes 1572872 | tf_op jit(solution)/shard_map/ppermute | solution.py:34
  175.1 264.7 %all-reduce.8.cloned.1.call-start = ((), (), s32[]{:S(2)}) async-start(), calls=%async_computation.2 | async-start | bytes 4194304 | tf_op jit(solution)/shard_map/psum | solution.py:20
  282.0 11.0 %copy-start.1 = (f32[4096,128]{1,0:T(8,128)S(1)}, f32[4096,128]{1,0:T(8,128)}, u32[]{:S(2)}) copy-start(f32[4096,128]{1,0:T(8,128)} %all-reduce.6.cloned.1.call-done) | copy-start | bytes 6291460
  289.1 2.0 collective-permute-start.2
  291.9 16.4 %collective-permute-start.3 = (f32[1024,128]{0,1:T(8,128)}, f32[1024,128]{0,1:T(8,128)}, u32[]{:S(2)}, u32[]{:S(2)}) collective-permute-start(f32[1024,128]{0,1:T(8,128)} %add.66), channel_id=1, source_target_pairs={{0,2},{1,3},{2,0},{3,1},{4,6},{5,7},{6,4},{7,5},{8,10},{9,11},{10,... | collective-permute-start | bytes 1572872 | tf_op jit(solution)/shard_map/ppermute | solution.py:34
  331.7 0.8 copy-start.3
  452.4 7.0 %copy-start.2 = (f32[4096,128]{1,0:T(8,128)}, f32[4096,128]{1,0:T(8,128)S(1)}, u32[]{:S(2)}) copy-start(f32[4096,128]{1,0:T(8,128)S(1)} %get-tuple-element.5) | copy-start | bytes 6291460
  459.5 40.3 %copy-start.4 = (f32[1024,128]{0,1:T(8,128)S(1)}, f32[1024,128]{0,1:T(8,128)}, u32[]{:S(2)}) copy-start(f32[1024,128]{0,1:T(8,128)} %copy-done.3) | copy-start | bytes 1572868
  459.5 2.0 collective-permute-start.4
  461.5 16.3 %collective-permute-start.5 = (f32[1024,128]{0,1:T(8,128)S(1)}, f32[1024,128]{0,1:T(8,128)}, u32[]{:S(2)}, u32[]{:S(2)}) collective-permute-start(f32[1024,128]{0,1:T(8,128)S(1)} %add.71), channel_id=1, source_target_pairs={{0,2},{1,3},{2,0},{3,1},{4,6},{5,7},{6,4},{7,5},{8,10},{9,11},{10,... | collective-permute-start | bytes 1572872 | tf_op jit(solution)/shard_map/ppermute | solution.py:34
Sparse Core Ops, SparseCore 0:
  14.5 104.4 all-reduce.3
  175.2 98.0 all-reduce.5
  340.7 99.0 all-reduce.7
